TPU v7x, 32 devices: a whole 2x2x4 slice. The times are simulated.
32 devices in a mesh: clips: 2 (over y), tm: 4 (over x, core), rows: 4 (over z).
Axes of the slice: x: 2, y: 2, z: 4, core: 2. Of those that a mesh axis runs over, the one named last changes fastest.
Arguments:
- features: bfloat16 [8, 8, 48, 384], P(('clips', 'tm'), 'rows'), parts along dimension 0, may hold values from -320 to 320
- first_gain: float32 [384], replicated, may hold values from 0.5 to 1.5
- first_shift: float32 [384], replicated, may hold values from -3 to 3
- first_kernel: bfloat16 [384, 3, 3, 3, 384], P('tm'), may hold values from -0.0625 to 0.0625
- first_bias: float32 [384], P('tm'), may hold values from -2 to 2
- second_gain: float32 [384], replicated, may hold values from 0.5 to 1.5
- second_shift: float32 [384], replicated, may hold values from -3 to 3
- second_kernel: bfloat16 [384, 3, 3, 3, 384], P('tm'), may hold values from -0.0625 to 0.0625
- second_bias: float32 [384], P('tm'), may hold values from -2 to 2
- third_gain: float32 [384], replicated, may hold values from 0.5 to 1.5
- third_shift: float32 [384], replicated, may hold values from -3 to 3
- query_weight: bfloat16 [384, 384], replicated, may hold values from -0.30618622 to 0.30618622
- key_weight: bfloat16 [384, 384], replicated, may hold values from -1.8371173 to 1.8371173
- value_weight: bfloat16 [384, 384], replicated, may hold values from -0.3125 to 0.3125
- output_weight: bfloat16 [384, 384], replicated, may hold values from -0.3125 to 0.3125
Outputs:
- decoded: bfloat16 [8, 8, 48, 384], P(('clips', 'tm'), 'rows'), parts along dimension 0
There are 2 independent parts, one for each index of `clips`. A program takes and returns all parts, laid end to end along the dimension named above; an argument that names none is the same for every part. Nothing has to cross between parts.
All inputs are finite; a program needn't handle non-finite values.
Results may differ from a plain program's by a relative error of at most 0.029.
Values may be sent and summed in bfloat16 or wider, within the bound.
A program may use at most 64 MiB of HBM per device.

v0:
```python
import functools

import jax
import jax.numpy as jnp
from jax import lax
from jax.experimental import pallas as pl
from jax.experimental.pallas import tpu as pltpu
from jax.sharding import PartitionSpec as P

GROUPS = 32
EPS = 1e-06
LANES = 128
MESH = pl.DeviceIdType.MESH
F32 = jnp.float32
BF16 = jnp.bfloat16
NT = (((1,), (1,)), ((), ()))


def flat(ref):
    return ref[...].reshape(1, ref.shape[0])


def padded(ref):
    row = flat(ref)
    rest = LANES - ref.shape[0]
    return jnp.concatenate([row, jnp.zeros((1, rest), F32)], axis=1) if rest else row


def each(count, body):
    if count <= 16:
        for n in range(count):
            body(n)
    else:
        lax.fori_loop(0, count, lambda n, c: (body(n), c)[1], 0)


def membership(size, per_group):
    a = lax.broadcasted_iota(jnp.int32, (size, size), 0) // per_group
    b = lax.broadcasted_iota(jnp.int32, (size, size), 1) // per_group
    return jnp.where(a == b, 1.0, 0.0).astype(BF16)


def group_sum(rows, member):
    hi = rows.astype(BF16).astype(F32)
    rest = rows - hi
    mid = rest.astype(BF16).astype(F32)
    low = rest - mid
    count = rows.shape[0]
    terms = jnp.concatenate([hi, mid, low], axis=0).astype(BF16)
    out = jnp.dot(terms, member, preferred_element_type=F32)
    return out[:count] + out[count : 2 * count] + out[2 * count :]


def block_stats(blocks, member, entries):
    sums = jnp.concatenate([jnp.sum(b, axis=0, keepdims=True) for b in blocks], axis=0)
    means = group_sum(sums, member) / entries
    squares = []
    for n, b in enumerate(blocks):
        d = b - means[n : n + 1]
        squares.append(jnp.sum(d * d, axis=0, keepdims=True))
    return means, group_sum(jnp.concatenate(squares, axis=0), member)


def merge_stats(means, squares, entries):
    count = len(means)
    mean = functools.reduce(lambda a, b: a + b, means) / count
    total = functools.reduce(lambda a, b: a + b, squares)
    for m in means:
        d = m - mean
        total = total + entries * (d * d)
    return mean, lax.rsqrt(total / (count * entries) + EPS)


def kernel(T, R, W, rows, C, OUT,
           feath, g1h, s1h, w1h, b1h, g2h, s2h, w2h, b2h, g3h, s3h, wqh, wkh, wvh, woh,
           out,
           feat, g1, s1, g2, s2, g3, s3, b1, b2, xin, y1, cols, w1, w2, aw, st1, st2, hs, hfull, normed,
           lsem, blk_s, blk_r, top_s, top_r, bot_s, bot_r, st_s, st_r, hid_s, hid_r):
    t = lax.axis_index("tm")
    z = lax.axis_index("rows")
    me = t * R + z
    N = T * R
    RP = rows * W
    EXT = (rows + 2) * W
    per = C // GROUPS
    entries = RP * per

    loads = [
        pltpu.make_async_copy(w1h, w1.at[:, pl.ds(0, OUT), :], lsem.at[0]),
        pltpu.make_async_copy(w2h, w2.at[:, pl.ds(0, OUT), :], lsem.at[1]),
    ] + [
        pltpu.make_async_copy(src, aw.at[n], lsem.at[2 + n])
        for n, src in enumerate((wqh, wkh, wvh, woh))
    ]
    small = [
        pltpu.make_async_copy(src, dst, lsem.at[6 + n])
        for n, (src, dst) in enumerate((
            (feath, feat), (g1h, g1), (s1h, s1), (g2h, g2), (s2h, s2), (g3h, g3), (s3h, s3),
            (b1h, b1), (b2h, b2)))
    ]
    for load in small + loads:
        load.start()

    def peer(p):
        other = lax.rem(me + p, N)
        return other // R, lax.rem(other, R)

    barrier = pltpu.get_barrier_semaphore()

    def greet(n):
        pt, pz = peer(n + 1)
        pl.semaphore_signal(barrier, inc=1, device_id={"tm": pt, "rows": pz}, device_id_type=MESH)

    each(N - 1, greet)

    def remote(src, dst, ssem, rsem, pt, pz):
        return pltpu.make_async_remote_copy(
            src_ref=src, dst_ref=dst, send_sem=ssem, recv_sem=rsem,
            device_id={"tm": pt, "rows": pz}, device_id_type=MESH)

    for load in small:
        load.wait()
    x = feat[...].astype(F32)
    member = membership(C, per)
    mean, square = block_stats([x], member, entries)
    st1[me] = jnp.concatenate([mean, square], axis=0)
    if OUT < LANES:
        w1[:, OUT:, :] = jnp.zeros((27, LANES - OUT, C), BF16)
        w2[:, OUT:, :] = jnp.zeros((27, LANES - OUT, C), BF16)

    pl.semaphore_wait(barrier, N - 1)

    def stat_copy(phase, ref, n):
        pt, pz = peer(n + 1)
        return remote(ref.at[me], ref.at[me], st_s.at[phase, n], st_r.at[phase, me], pt, pz)

    def stat_arrival(phase, ref, n):
        pt, pz = peer(n + 1)
        src = pt * R + pz
        return remote(ref.at[src], ref.at[src], st_s.at[phase, n], st_r.at[phase, src], pt, pz)

    core = lax.rem(t, 2)
    sib = t + 1 - 2 * core
    X = T // 2
    chip = t // 2

    def same(n):
        return 2 * lax.rem(chip + n, X) + core

    def other(n):
        return 2 * lax.rem(chip + n, X) + 1 - core

    def pieces(phase, body, first, last, at):
        blocks = [remote(body, at(t, W, RP), blk_s.at[phase, n], blk_r.at[phase, t], same(n), z)
                  for n in range(1, X)]
        blocks.append(remote(body, at(t, W, RP), blk_s.at[phase, 0], blk_r.at[phase, t], sib, z))
        down = [remote(last, at(t, 0, W), top_s.at[phase, n], top_r.at[phase, t], same(n), z + 1)
                for n in range(X)]
        up = [remote(first, at(t, W + RP, W), bot_s.at[phase, n], bot_r.at[phase, t], same(n), z - 1)
              for n in range(X)]
        return blocks, down, up

    def gather_start(*args):
        blocks, down, up = pieces(*args)
        for c in blocks:
            c.start()

        @pl.when(z + 1 < R)
        def _():
            for c in down[1:] + down[:1]:
                c.start()

        @pl.when(z > 0)
        def _():
            for c in up[1:] + up[:1]:
                c.start()

    def forward(phase, at, sems, offset, count, src, n):
        ssem, rsem = sems
        return remote(at(src, offset, count), at(src, offset, count),
                      ssem.at[phase, X + n], rsem.at[phase, src], sib, z)

    blk, top, bot = (blk_s, blk_r), (top_s, top_r), (bot_s, bot_r)
    forwards = ((blk, W, RP, 1), (top, 0, W, 0), (bot, W + RP, W, 0))

    def relay(phase, at, which):
        sems, offset, count, start = forwards[which]
        for n in range(start, X):
            c = forward(phase, at, sems, offset, count, same(n), n)
            c.wait_recv()
            c.start()

    def sibling_wait(phase, at, which):
        sems, offset, count, _ = forwards[which]
        for n in range(X):
            forward(phase, at, sems, offset, count, other(n), n).wait_recv()

    def gather_sent(*args):
        phase, at = args[0], args[4]
        blocks, down, up = pieces(*args)
        for c in blocks:
            c.wait_send()
        for n in range(1, X):
            forward(phase, at, blk, W, RP, same(n), n).wait_send()

        @pl.when(z + 1 < R)
        def _():
            for c in down:
                c.wait_send()
            for n in range(X):
                forward(phase, at, bot, W + RP, W, same(n), n).wait_send()

        @pl.when(z > 0)
        def _():
            for c in up:
                c.wait_send()
            for n in range(X):
                forward(phase, at, top, 0, W, same(n), n).wait_send()

    def put_columns(f, offset, value):
        count = value.shape[0]
        active = value * (0.5 * jnp.tanh(0.5 * value) + 0.5)
        col = lax.rem(lax.broadcasted_iota(jnp.int32, (count, C), 0), W)
        before = jnp.where(col == 0, 0.0, pltpu.roll(active, 1, 0))
        after = jnp.where(col == W - 1, 0.0, pltpu.roll(active, count - 1, 0))
        cols[f, pl.ds(offset, count), 0:C] = before.astype(BF16)
        cols[f, pl.ds(offset, count), C : 2 * C] = active.astype(BF16)
        cols[f, pl.ds(offset, count), 2 * C : 3 * C] = after.astype(BF16)

    def conv(weights):
        parts = {}
        for i in range(3):
            frames = T - (2 - i)
            if frames <= 0:
                continue
            total = None
            for j in range(3):
                for k in range(3):
                    window = cols[0:frames, j * W : j * W + RP, k * C : (k + 1) * C]
                    term = lax.dot_general(
                        window.reshape(frames * RP, C), weights[(i * 3 + j) * 3 + k], NT,
                        preferred_element_type=F32)
                    total = term if total is None else total + term
            parts[i] = total
        results = []
        for f in range(T):
            value = parts[2][f * RP : (f + 1) * RP]
            for i in (0, 1):
                src = f + i - 2
                if src >= 0:
                    value = value + parts[i][src * RP : (src + 1) * RP]
            results.append(value)
        return results

    zero_row = jnp.zeros((W, 3 * C), BF16)

    at1 = lambda src, offset, count: xin.at[src, pl.ds(offset, count), :]
    phase1 = (0, feat, feat.at[pl.ds(0, W), :], feat.at[pl.ds(RP - W, W), :], at1)
    each(N - 1, lambda n: stat_copy(0, st1, n).start())
    gather_start(*phase1)
    xin[t, W : W + RP, :] = feat[...]
    each(N - 1, lambda n: stat_arrival(0, st1, n).wait_recv())

    gain1, shift1 = flat(g1), flat(s1)

    def norm1(f):
        means = [st1[f * R + r, 0:1, :] for r in range(R)]
        squares = [st1[f * R + r, 1:2, :] for r in range(R)]
        mean, inv = merge_stats(means, squares, entries)
        return mean, inv * gain1

    def fill1(f, offset, count):
        mean, scale = norm1(f)
        value = (xin[f, pl.ds(offset, count), :].astype(F32) - mean) * scale + shift1
        put_columns(f, offset, value)

    fill1(t, W, RP)
    relay(0, at1, 0)

    @pl.when(z > 0)
    def _():
        relay(0, at1, 1)

    @pl.when(z + 1 < R)
    def _():
        relay(0, at1, 2)

    for n in range(1, X):
        fill1(same(n), W, RP)
    sibling_wait(0, at1, 0)
    for n in range(X):
        fill1(other(n), W, RP)

    @pl.when(z > 0)
    def _():
        sibling_wait(0, at1, 1)
        for f in range(T):
            fill1(f, 0, W)

    @pl.when(z == 0)
    def _():
        for f in range(T):
            cols[f, 0:W, :] = zero_row

    @pl.when(z + 1 < R)
    def _():
        sibling_wait(0, at1, 2)
        for f in range(T):
            fill1(f, W + RP, W)

    @pl.when(z + 1 == R)
    def _():
        for f in range(T):
            cols[f, W + RP : EXT, :] = zero_row

    loads[0].wait()
    bias1 = padded(b1)
    outs = [(v + bias1).astype(BF16) for v in conv(w1)]
    member_out = membership(LANES, per)
    for f in range(T):
        y1[t, f, W : W + RP, :] = outs[f]
    mean, square = block_stats([v.astype(F32) for v in outs], member_out, entries)
    st2[me, 0] = mean
    st2[me, 1] = square

    at2 = lambda src, offset, count: y1.at[src, :, pl.ds(offset, count), :]
    phase2 = (1, at2(t, W, RP), at2(t, W, W), at2(t, RP, W), at2)
    each(N - 1, lambda n: stat_copy(1, st2, n).start())
    gather_start(*phase2)

    pick = jnp.where(
        (lax.broadcasted_iota(jnp.int32, (C, LANES), 0)
         == t * OUT + lax.broadcasted_iota(jnp.int32, (C, LANES), 1))
        & (lax.broadcasted_iota(jnp.int32, (C, LANES), 1) < OUT), 1.0, 0.0).astype(BF16)
    own = jnp.dot(xin[:, W : W + RP, :].reshape(T * RP, C), pick, preferred_element_type=F32)

    each(N - 1, lambda n: stat_arrival(1, st2, n).wait_recv())
    gain2, shift2 = flat(g2), flat(s2)
    mean_cols, inv_cols = [], []
    for s in range(T):
        mean, inv = merge_stats(
            [st2[s * R + r, 0] for r in range(R)], [st2[s * R + r, 1] for r in range(R)], entries)
        mean_cols.append(mean[:, :OUT])
        inv_cols.append(inv[:, :OUT])
    mean2 = jnp.concatenate(mean_cols, axis=1)
    scale2 = jnp.concatenate(inv_cols, axis=1) * gain2

    def joined(blocks):
        return jnp.concatenate([b.astype(F32)[:, :OUT] for b in blocks], axis=1)

    def fill2(f, offset, count):
        raw = joined([y1[s, f, offset : offset + count, :] for s in range(T)])
        value = (raw - mean2[f : f + 1]) * scale2[f : f + 1] + shift2
        put_columns(f, offset, value)

    relay(1, at2, 0)

    @pl.when(z > 0)
    def _():
        relay(1, at2, 1)

    @pl.when(z + 1 < R)
    def _():
        relay(1, at2, 2)

    sibling_wait(1, at2, 0)
    for f in range(T):
        fill2(f, W, RP)

    @pl.when(z > 0)
    def _():
        sibling_wait(1, at2, 1)
        for f in range(T):
            fill2(f, 0, W)

    @pl.when(z + 1 < R)
    def _():
        sibling_wait(1, at2, 2)
        for f in range(T):
            fill2(f, W + RP, W)

    loads[1].wait()
    bias2 = padded(b2)
    for f, v in enumerate(conv(w2)):
        rounded = (v + bias2).astype(BF16).astype(F32)
        hs[f] = (own[f * RP : (f + 1) * RP] + rounded).astype(BF16)

    def place(src, zz):
        return hfull.at[src, pl.ds(pl.multiple_of(zz * RP, 16), RP), :]

    def hidden_copy(n):
        pt, pz = peer(n + 1)
        return remote(hs.at[pt], place(t, z), hid_s.at[n], hid_r.at[me], pt, pz)

    def hidden_arrival(n):
        pt, pz = peer(n + 1)
        return remote(place(pt, pz), place(pt, pz), hid_s.at[n], hid_r.at[pt * R + pz], pt, pz)

    each(N - 1, lambda n: hidden_copy(n).start())
    hfull[t, pl.ds(pl.multiple_of(z * RP, 16), RP), :] = hs[t]

    each(N - 1, lambda n: stat_copy(0, st1, n).wait_send())
    gather_sent(*phase1)
    each(N - 1, lambda n: stat_copy(1, st2, n).wait_send())
    gather_sent(*phase2)
    for n in range(2, 6):
        loads[n].wait()

    each(N - 1, lambda n: hidden_arrival(n).wait_recv())

    total_rows = R * RP
    chunk = min(total_rows, 4 * RP)
    parts = total_rows // chunk

    def frame_rows(n):
        start = pl.multiple_of(n * chunk, 16)
        return joined([hfull[s, pl.ds(start, chunk), :] for s in range(T)])

    def fold(body, init):
        if parts == 1:
            return body(0, init)
        return lax.fori_loop(0, parts, body, init)

    zero = jnp.zeros((1, C), F32)
    sums = fold(lambda n, a: a + jnp.sum(frame_rows(n), axis=0, keepdims=True), zero)
    mean = group_sum(sums, member) / (entries * R)

    def deviation(n, a):
        d = frame_rows(n) - mean
        return a + jnp.sum(d * d, axis=0, keepdims=True)

    var = group_sum(fold(deviation, zero), member) / (entries * R)
    scale3 = lax.rsqrt(var + EPS) * flat(g3)
    shift3 = flat(s3)

    def normalise(n, c):
        start = pl.multiple_of(n * chunk, 16)
        value = ((frame_rows(n) - mean) * scale3 + shift3).astype(BF16)
        normed[0, pl.ds(start, chunk), :] = value
        normed[1, pl.ds(start, chunk), :] = jnp.dot(value, aw[1], preferred_element_type=F32).astype(BF16)
        normed[2, pl.ds(start, chunk), :] = jnp.dot(value, aw[2], preferred_element_type=F32).astype(BF16)
        return c

    fold(normalise, 0)
    mine = pl.ds(pl.multiple_of(z * RP, 16), RP)
    queries = (jnp.dot(normed[0, mine, :], aw[0], preferred_element_type=F32) * C ** (-0.5)).astype(BF16)
    scores = lax.dot_general(queries, normed[1], NT, preferred_element_type=F32)
    peak = jnp.max(scores, axis=1, keepdims=True)
    weights = jnp.exp(scores - peak)
    total = jnp.sum(weights, axis=1, keepdims=True)
    summed = jnp.dot(weights.astype(BF16), normed[2], preferred_element_type=F32)
    attended = (summed / total).astype(BF16)
    hidden = joined([hfull[s, mine, :] for s in range(T)])
    out[...] = (hidden + jnp.dot(attended, aw[3], preferred_element_type=F32)).astype(BF16)

    each(N - 1, lambda n: hidden_copy(n).wait_send())


def solution(mesh):
    T, R = mesh.shape["tm"], mesh.shape["rows"]

    def per_device(features, g1, s1, k1, b1, g2, s2, k2, b2, g3, s3, wq, wk, wv, wo):
        _, rows, W, C = features.shape
        OUT = k1.shape[0]
        RP, EXT, N = rows * W, (rows + 2) * W, T * R
        taps = lambda k: jnp.transpose(k, (1, 2, 3, 0, 4)).reshape(27, OUT, C)
        vmem = pl.BlockSpec(memory_space=pltpu.VMEM)
        hbm = pl.BlockSpec(memory_space=pltpu.HBM)
        dma = pltpu.SemaphoreType.DMA
        result = pl.pallas_call(
            functools.partial(kernel, T, R, W, rows, C, OUT),
            out_shape=jax.ShapeDtypeStruct((RP, C), BF16),
            in_specs=[hbm] * 15,
            out_specs=vmem,
            scratch_shapes=[pltpu.VMEM((RP, C), BF16)] + [pltpu.VMEM((C,), F32)] * 6
            + [pltpu.VMEM((OUT,), F32)] * 2 + [
                pltpu.VMEM((T, EXT, C), BF16),
                pltpu.VMEM((T, T, EXT, LANES), BF16),
                pltpu.VMEM((T, EXT, 3 * C), BF16),
                pltpu.VMEM((27, LANES, C), BF16),
                pltpu.VMEM((27, LANES, C), BF16),
                pltpu.VMEM((4, C, C), BF16),
                pltpu.VMEM((N, 2, C), F32),
                pltpu.VMEM((N, 2, T, LANES), F32),
                pltpu.VMEM((T, RP, LANES), BF16),
                pltpu.VMEM((T, R * RP, LANES), BF16),
                pltpu.VMEM((3, R * RP, C), BF16),
                dma((15,)),
                dma((2, T)), dma((2, T)),
                dma((2, T)), dma((2, T)),
                dma((2, T)), dma((2, T)),
                dma((2, N)), dma((2, N)),
                dma((N,)), dma((N,)),
            ],
            compiler_params=pltpu.CompilerParams(
                collective_id=0, has_side_effects=True, vmem_limit_bytes=62 * 1024 * 1024),
        )(features.reshape(RP, C), g1, s1, taps(k1), b1, g2, s2,
          taps(k2), b2, g3, s3, wq, wk, wv, wo)
        return result.reshape(features.shape)

    in_specs = (
        P(("clips", "tm"), "rows", None, None), P(), P(),
        P("tm", None, None, None, None), P("tm"), P(), P(),
        P("tm", None, None, None, None), P("tm"), P(), P(), P(), P(), P(), P(),
    )
    return jax.shard_map(
        per_device, mesh=mesh, in_specs=in_specs,
        out_specs=P(("clips", "tm"), "rows", None, None), check_vma=False)
```

profile of v0, /device:TPU:0, one launch (start us, length us, event | category | flops | bytes accessed | tf_op | source)
XLA Modules:
  0.0 40.5 jit_solution(6317948326270687304)
XLA Ops:
  0.0 39.0 %shard_map.145 = bf16[96,384]{1,0:T(8,128)(2,1)} custom-call(bf16[96,384]{1,0:T(8,128)(2,1)} %bitcast.11, f32[384]{0:T(512)} %g1h.1, f32[384]{0:T(512)} %s1h.1, bf16[27,96,384]{2,1,0:T(8,128)(2,1)} %bitcast.8, f32[96]{0:T(128)} %b1h.1, f32[384]{0:T(512)} %g2h.1, f32[384]{0:T(512)} %s2h.1, bf16[27,96,384]{2,1,0:T(8,128)(2,1)} %bitcast.9, f32[96]{0:T(128)} %b2h.1, ...), custom_call_target="tpu_custom_call" | custom-call | tf_op jit(solution)/shard_map/pallas_call | solution.py:470
  39.0 1.5 %copy.17 = bf16[1,2,48,384]{3,2,1,0:T(8,128)(2,1)} copy(bf16[1,2,48,384]{3,2,1,0:T(8,128)(2,1)} %bitcast.10) | data formatting | bytes 147456
where the time goes:
time: 40.7 us; the launch traced here: 40.5 us
  Pallas kernels  39 us (96%)
  local copies, waits for them, and re-layouts  1.52 us (4%)
    pallas_call x1, Pallas kernels, per_device(): pl.pallas_call(functools.partial(kernel, T, R, W, rows, C, OUT), out_shap...  39 us
    unnamed x1, local copies, waits for them, and re-layouts  1.52 us

commit v1 on v0

--- a/solution.py
+++ b/solution.py
@@ -469,7 +469,7 @@
         dma = pltpu.SemaphoreType.DMA
         result = pl.pallas_call(
             functools.partial(kernel, T, R, W, rows, C, OUT),
-            out_shape=jax.ShapeDtypeStruct((RP, C), BF16),
+            out_shape=pltpu.VMEM((RP, C), BF16),
             in_specs=[hbm] * 15,
             out_specs=vmem,
             scratch_shapes=[pltpu.VMEM((RP, C), BF16)] + [pltpu.VMEM((C,), F32)] * 6

time: 40.7 us -> 39.2 us (0.963)
  local copies, waits for them, and re-layouts: 1.52 us -> 0.64 us
  Pallas kernels: 39 us -> 38.4 us
    unnamed x1, local copies, waits for them, and re-layouts: 1.52 us -> 0.64 us
    pallas_call x1, Pallas kernels: 39 us -> 38.4 us  [per_device(): pl.pallas_call(functools.partial(kernel, T, R, W, rows, C, OUT), out_shap...]
where the time goes in v1:
time: 39.2 us; the launch traced here: 39.1 us
  Pallas kernels  38.4 us (98%)
  local copies, waits for them, and re-layouts  0.64 us (2%)
    pallas_call x1, Pallas kernels, per_device(): pl.pallas_call(functools.partial(kernel, T, R, W, rows, C, OUT), out_shap...  38.4 us

profile of v1, /device:TPU:0, one launch (start us, length us, event | category | flops | bytes accessed | tf_op | source)
XLA Modules:
  0.0 39.1 jit_solution(2123339253346388556)
XLA Ops:
  0.0 38.4 %shard_map.145 = bf16[96,384]{1,0:T(8,128)(2,1)S(1)} custom-call(bf16[96,384]{1,0:T(8,128)(2,1)} %bitcast.11, f32[384]{0:T(512)} %g1h.1, f32[384]{0:T(512)} %s1h.1, bf16[27,96,384]{2,1,0:T(8,128)(2,1)} %bitcast.9, f32[96]{0:T(128)} %b1h.1, f32[384]{0:T(512)} %g2h.1, f32[384]{0:T(512)} %s2h.1, bf16[27,96,384]{2,1,0:T(8,128)(2,1)} %bitcast.10, f32[96]{0:T(128)} %b2h.1, ...), custom_call_target="tpu_custom_call" | custom-call | tf_op jit(solution)/shard_map/pallas_call | solution.py:470
  38.4 0.6 %copy.17 = bf16[1,2,48,384]{3,2,1,0:T(8,128)(2,1)} copy(bf16[1,2,48,384]{3,2,1,0:T(8,128)(2,1)S(1)} %bitcast.8) | data formatting | bytes 147456

commit v2 on v1

v2 whole, which is shorter than its diff:
```python
import functools

import jax
import jax.numpy as jnp
from jax import lax
from jax.experimental import pallas as pl
from jax.experimental.pallas import tpu as pltpu
from jax.sharding import PartitionSpec as P

GROUPS = 32
EPS = 1e-06
LANES = 128
MESH = pl.DeviceIdType.MESH
F32 = jnp.float32
BF16 = jnp.bfloat16
NT = (((1,), (1,)), ((), ()))


def flat(ref):
    return ref[...].reshape(1, ref.shape[0])


def padded(ref):
    row = flat(ref)
    rest = LANES - ref.shape[0]
    return jnp.concatenate([row, jnp.zeros((1, rest), F32)], axis=1) if rest else row


def each(count, body):
    if count <= 16:
        for n in range(count):
            body(n)
    else:
        lax.fori_loop(0, count, lambda n, c: (body(n), c)[1], 0)


def membership(size, per_group):
    a = lax.broadcasted_iota(jnp.int32, (size, size), 0) // per_group
    b = lax.broadcasted_iota(jnp.int32, (size, size), 1) // per_group
    return jnp.where(a == b, 1.0, 0.0).astype(BF16)


def group_sum(rows, member):
    hi = rows.astype(BF16).astype(F32)
    rest = rows - hi
    mid = rest.astype(BF16).astype(F32)
    low = rest - mid
    count = rows.shape[0]
    terms = jnp.concatenate([hi, mid, low], axis=0).astype(BF16)
    out = jnp.dot(terms, member, preferred_element_type=F32)
    return out[:count] + out[count : 2 * count] + out[2 * count :]


def block_stats(blocks, member, entries):
    sums = jnp.concatenate([jnp.sum(b, axis=0, keepdims=True) for b in blocks], axis=0)
    means = group_sum(sums, member) / entries
    squares = []
    for n, b in enumerate(blocks):
        d = b - means[n : n + 1]
        squares.append(jnp.sum(d * d, axis=0, keepdims=True))
    return means, group_sum(jnp.concatenate(squares, axis=0), member)


def merge_stats(means, squares, entries):
    count = len(means)
    mean = functools.reduce(lambda a, b: a + b, means) / count
    total = functools.reduce(lambda a, b: a + b, squares)
    for m in means:
        d = m - mean
        total = total + entries * (d * d)
    return mean, lax.rsqrt(total / (count * entries) + EPS)


def lanes_of(count):
    return lax.broadcasted_iota(jnp.int32, (count, LANES), 1)


def pack_rows(v):
    tail = v[80:96]
    lane = lanes_of(16)
    parts = []
    for j in range(3):
        moved = pltpu.roll(tail, 96 - 32 * j, 1)
        parts.append(jnp.where(lane >= 96, moved, v[16 * j : 16 * j + 16]))
    return jnp.concatenate(parts + [v[48:80]], axis=0)


def unpack_rows(p):
    lane = lanes_of(16)
    tail = jnp.zeros((16, LANES), F32)
    for j in range(3):
        moved = pltpu.roll(p[16 * j : 16 * j + 16], 32 + 32 * j, 1)
        tail = jnp.where((lane >= 32 * j) & (lane < 32 * j + 32), moved, tail)
    return jnp.concatenate([p, tail], axis=0)


def kernel(T, R, W, rows, C, OUT,
           feath, g1h, s1h, w1h, b1h, g2h, s2h, w2h, b2h, g3h, s3h, wqh, wkh, wvh, woh,
           out,
           feat, g1, s1, g2, s2, g3, s3, b1, b2, xin, y1, cols, w1, w2, aw, st1, st2, st3, hs, hfull, hid, normed, mix, pairs, singles,
           lsem, snd, rcv, st_s, st_r, hid_s, hid_r):
    t = lax.axis_index("tm")
    z = lax.axis_index("rows")
    me = t * R + z
    N = T * R
    RP = rows * W
    EXT = (rows + 2) * W
    per = C // GROUPS
    entries = RP * per
    packed2 = y1.shape[1] < T
    packed3 = hs.shape[1] < RP

    def peer(p):
        other = lax.rem(me + p, N)
        return other // R, lax.rem(other, R)

    barrier = pltpu.get_barrier_semaphore()

    def greet(n):
        pt, pz = peer(n + 1)
        pl.semaphore_signal(barrier, inc=1, device_id={"tm": pt, "rows": pz}, device_id_type=MESH)

    small = [
        pltpu.make_async_copy(src, dst, lsem.at[n])
        for n, (src, dst) in enumerate((
            (feath, feat), (g1h, g1), (s1h, s1), (g2h, g2), (s2h, s2), (g3h, g3), (s3h, s3),
            (b1h, b1), (b2h, b2)))
    ]
    small[0].start()
    each(N - 1, greet)
    for load in small[1:]:
        load.start()

    def load_taps(src, dst, n):
        for i in range(3):
            for k in range(3):
                pltpu.make_async_copy(
                    src.at[i, :, k], dst.at[:, 2 - i, pl.ds(0, OUT), pl.ds(k * C, C)], lsem.at[n]).start()

    def taps_loaded(dst, n):
        whole = dst.at[:, :, pl.ds(0, OUT), :]
        pltpu.make_async_copy(whole, whole, lsem.at[n]).wait()

    load_taps(w1h, w1, 9)
    for n, src in enumerate((wqh, wkh, wvh, woh)):
        pltpu.make_async_copy(src, aw.at[n], lsem.at[11]).start()
    load_taps(w2h, w2, 10)

    def remote(src, dst, ssem, rsem, pt, pz):
        return pltpu.make_async_remote_copy(
            src_ref=src, dst_ref=dst, send_sem=ssem, recv_sem=rsem,
            device_id={"tm": pt, "rows": pz}, device_id_type=MESH)

    small[0].wait()
    x = feat[...].astype(F32)
    member = membership(C, per)
    mean, square = block_stats([x], member, entries)
    st1[me] = jnp.concatenate([mean, square], axis=0)
    for load in small[1:]:
        load.wait()
    if OUT < LANES:
        w1[:, :, OUT:, :] = jnp.zeros((3, 3, LANES - OUT, 3 * C), BF16)
        w2[:, :, OUT:, :] = jnp.zeros((3, 3, LANES - OUT, 3 * C), BF16)

    pl.semaphore_wait(barrier, N - 1)

    def stat_copy(phase, ref, n):
        pt, pz = peer(n + 1)
        return remote(ref.at[me], ref.at[me], st_s.at[phase], st_r.at[phase], pt, pz)

    def stat_all(phase, ref):
        most = ref.at[pl.ds(0, N - 1)]
        return remote(most, most, st_s.at[phase], st_r.at[phase], lax.rem(t + 1, T), z)

    core = lax.rem(t, 2)
    sib = t + 1 - 2 * core
    X = T // 2
    chip = t // 2

    def same(n):
        return 2 * lax.rem(chip + n, X) + core

    def other(n):
        return 2 * lax.rem(chip + n, X) + 1 - core

    BLK, TOP, BOT = 0, 1, 2
    DOWN, UP = 1, 2
    spans = ((W, RP), (0, W), (W + RP, W))

    def gather_start(phase, body, first, last, at):
        for n in range(1, X):
            remote(body, at(t, W, RP), snd.at[phase, 0], rcv.at[phase, BLK, t], same(n), z).start()
        remote(body, at(t, W, RP), snd.at[phase, 0], rcv.at[phase, BLK, t], sib, z).start()
        order = list(range(1, X)) + [0]

        @pl.when(z + 1 < R)
        def _():
            for n in order:
                remote(last, at(t, 0, W), snd.at[phase, DOWN], rcv.at[phase, TOP, t], same(n), z + 1).start()

        @pl.when(z > 0)
        def _():
            for n in order:
                remote(first, at(t, W + RP, W), snd.at[phase, UP], rcv.at[phase, BOT, t], same(n), z - 1).start()

    def forward(phase, at, which, src):
        sem = (0, UP, DOWN)[which]
        block = at(src, *spans[which])
        return remote(block, block, snd.at[phase, sem], rcv.at[phase, which, src], sib, z)

    def relay(phase, at, which, sources):
        for n in sources:
            c = forward(phase, at, which, same(n))
            c.wait_recv()
            c.start()

    def relay_rims(phase, at, sources):
        @pl.when(z > 0)
        def _():
            relay(phase, at, TOP, sources)

        @pl.when(z + 1 < R)
        def _():
            relay(phase, at, BOT, sources)

    def sibling_wait(phase, at, which):
        for n in range(X):
            forward(phase, at, which, other(n)).wait_recv()

    def gather_sent(phase, at, span_at):
        def done(block, sem):
            remote(block, block, snd.at[phase, sem], rcv.at[phase, BLK, t], sib, z).wait_send()

        done(span_at(T - 1, W, RP), 0)

        @pl.when(z + 1 < R)
        def _():
            done(span_at(T, 0, W), DOWN)

        @pl.when(z > 0)
        def _():
            done(span_at(T, 0, W), UP)

    def put_columns(f, offset, value):
        count = value.shape[0]
        active = value * (0.5 * jnp.tanh(0.5 * value) + 0.5)
        col = lax.rem(lax.broadcasted_iota(jnp.int32, (count, C), 0), W)
        before = jnp.where(col == 0, 0.0, pltpu.roll(active, 1, 0))
        after = jnp.where(col == W - 1, 0.0, pltpu.roll(active, count - 1, 0))
        cols[f, pl.ds(offset, count), 0:C] = before.astype(BF16)
        cols[f, pl.ds(offset, count), C : 2 * C] = active.astype(BF16)
        cols[f, pl.ds(offset, count), 2 * C : 3 * C] = after.astype(BF16)

    def conv(weights, taps, before):
        pair, single = before
        for j in taps:
            window = cols[:, j * W : j * W + RP, :].reshape(T * RP, 3 * C)
            term = lax.dot_general(
                window, weights[j, 0:2].reshape(2 * LANES, 3 * C), NT, preferred_element_type=F32)
            pair = term if pair is None else pair + term
            if T > 2:
                term = lax.dot_general(
                    window[: (T - 2) * RP], weights[j, 2], NT, preferred_element_type=F32)
                single = term if single is None else single + term
        return pair, single

    def keep(sums):
        pairs[...] = sums[0]
        if T > 2:
            singles[...] = sums[1]

    def kept():
        return pairs[...], (singles[...] if T > 2 else None)

    def conv_frames(pair, single):
        results = []
        for f in range(T):
            value = pair[f * RP : (f + 1) * RP, :LANES]
            if f >= 1:
                value = value + pair[(f - 1) * RP : f * RP, LANES:]
            if f >= 2:
                value = value + single[(f - 2) * RP : (f - 1) * RP]
            results.append(value)
        return results

    zero_row = jnp.zeros((W, 3 * C), BF16)

    at1 = lambda src, offset, count: xin.at[src, pl.ds(offset, count), :]
    many1 = lambda count, offset, size: xin.at[pl.ds(0, count), pl.ds(offset, size), :]
    each(N - 1, lambda n: stat_copy(0, st1, n).start())
    gather_start(0, feat, feat.at[pl.ds(0, W), :], feat.at[pl.ds(RP - W, W), :], at1)
    xin[t, W : W + RP, :] = feat[...]
    stat_all(0, st1).wait_recv()

    gain1, shift1 = flat(g1), flat(s1)

    def norm1(f):
        means = [st1[f * R + r, 0:1, :] for r in range(R)]
        squares = [st1[f * R + r, 1:2, :] for r in range(R)]
        mean, inv = merge_stats(means, squares, entries)
        return mean, inv * gain1

    def fill1(f, offset, count):
        mean, scale = norm1(f)
        value = (xin[f, pl.ds(offset, count), :].astype(F32) - mean) * scale + shift1
        put_columns(f, offset, value)

    fill1(t, W, RP)
    relay(0, at1, BLK, range(1, X))
    for n in range(1, X):
        fill1(same(n), W, RP)
    relay_rims(0, at1, (0,))
    relay_rims(0, at1, range(1, X))
    sibling_wait(0, at1, BLK)
    for n in range(X):
        fill1(other(n), W, RP)

    taps_loaded(w1, 9)
    keep(conv(w1, (1,), (None, None)))

    @pl.when(z > 0)
    def _():
        sibling_wait(0, at1, TOP)
        for f in range(T):
            fill1(f, 0, W)

    @pl.when(z == 0)
    def _():
        for f in range(T):
            cols[f, 0:W, :] = zero_row

    @pl.when(z + 1 < R)
    def _():
        sibling_wait(0, at1, BOT)
        for f in range(T):
            fill1(f, W + RP, W)

    @pl.when(z + 1 == R)
    def _():
        for f in range(T):
            cols[f, W + RP : EXT, :] = zero_row

    bias1 = padded(b1)
    acc = conv(w1, (0, 2), kept())
    outs = [(v + bias1).astype(BF16).astype(F32) for v in conv_frames(*acc)]
    member_out = membership(LANES, per)
    if packed2:
        lane = lanes_of(RP)
        for f in range(T - 1):
            moved = pltpu.roll(outs[T - 1], 96 - 32 * f, 1)
            y1[t, f, W : W + RP, :] = jnp.where(lane >= 96, moved, outs[f]).astype(BF16)
    else:
        for f in range(T):
            y1[t, f, W : W + RP, :] = outs[f].astype(BF16)

    at2 = lambda src, offset, count: y1.at[src, :, pl.ds(offset, count), :]
    many2 = lambda count, offset, size: y1.at[pl.ds(0, count), :, pl.ds(offset, size), :]
    mean, square = block_stats(outs, member_out, entries)
    st2[me, 0] = mean
    st2[me, 1] = square
    each(N - 1, lambda n: stat_copy(1, st2, n).start())
    gather_start(1, at2(t, W, RP), at2(t, W, W), at2(t, RP, W), at2)

    pick = jnp.where(
        (lax.broadcasted_iota(jnp.int32, (C, LANES), 0)
         == t * OUT + lax.broadcasted_iota(jnp.int32, (C, LANES), 1))
        & (lax.broadcasted_iota(jnp.int32, (C, LANES), 1) < OUT), 1.0, 0.0).astype(BF16)
    own = jnp.dot(xin[:, W : W + RP, :].reshape(T * RP, C), pick, preferred_element_type=F32)
    pltpu.make_async_copy(aw, aw, lsem.at[11]).wait()
    mix[0] = (lax.dot_general(aw[0], aw[1], NT, preferred_element_type=F32) * C ** (-0.5)).astype(BF16)
    mix[1] = jnp.dot(aw[2], aw[3], preferred_element_type=F32).astype(BF16)

    stat_all(1, st2).wait_recv()
    gain2, shift2 = flat(g2), flat(s2)
    mean_cols, inv_cols = [], []
    for s in range(T):
        mean, inv = merge_stats(
            [st2[s * R + r, 0] for r in range(R)], [st2[s * R + r, 1] for r in range(R)], entries)
        mean_cols.append(mean[:, :OUT])
        inv_cols.append(inv[:, :OUT])
    mean2 = jnp.concatenate(mean_cols, axis=1)
    scale2 = jnp.concatenate(inv_cols, axis=1) * gain2

    def joined(blocks):
        return jnp.concatenate([b[:, :OUT] for b in blocks], axis=1)

    def conv_out(s, f, offset, count):
        if not packed2 or f < T - 1:
            return y1[s, f, offset : offset + count, :].astype(F32)
        lane = lanes_of(count)
        value = None
        for j in range(3):
            moved = pltpu.roll(y1[s, j, offset : offset + count, :].astype(F32), 32 + 32 * j, 1)
            value = moved if value is None else jnp.where(lane >= 32 * j, moved, value)
        return value

    def fill2(f, offset, count):
        raw = joined([conv_out(s, f, offset, count) for s in range(T)])
        value = (raw - mean2[f : f + 1]) * scale2[f : f + 1] + shift2
        put_columns(f, offset, value)

    relay_rims(1, at2, (0,))
    relay(1, at2, BLK, range(1, X))
    relay_rims(1, at2, range(1, X))
    sibling_wait(1, at2, BLK)
    for f in range(T):
        fill2(f, W, RP)
    taps_loaded(w2, 10)
    keep(conv(w2, (1,), (None, None)))

    @pl.when(z > 0)
    def _():
        sibling_wait(1, at2, TOP)
        for f in range(T):
            fill2(f, 0, W)

    @pl.when(z + 1 < R)
    def _():
        sibling_wait(1, at2, BOT)
        for f in range(T):
            fill2(f, W + RP, W)

    bias2 = padded(b2)
    acc = conv(w2, (0, 2), kept())
    for f, v in enumerate(conv_frames(*acc)):
        rounded = (v + bias2).astype(BF16).astype(F32)
        value = own[f * RP : (f + 1) * RP] + rounded
        hs[f] = (pack_rows(value) if packed3 else value).astype(BF16)

    def place(zz, tt):
        return hfull.at[zz * T + tt]

    def group(zz, count):
        return hfull.at[pl.ds(zz * T, count)]

    def hidden_start(pt, pz):
        remote(hs.at[pt], place(z, t), hid_s.at[0], hid_r.at[z], pt, pz).start()

    if R <= 4:
        for d in range(R - 1, 0, -1):
            for there in (z + d, z - d):
                @pl.when((there >= 0) & (there < R))
                def _():
                    for n in range(T):
                        hidden_start(lax.rem(t + n, T), there)
        for n in range(1, T):
            hidden_start(lax.rem(t + n, T), z)
    else:
        each(N - 1, lambda n: hidden_start(*peer(n + 1)))
    hfull[z * T + t] = hs[t]

    stat_all(0, st1).wait_send()
    gather_sent(0, at1, many1)
    stat_all(1, st2).wait_send()
    gather_sent(1, at2, many2)

    def arrived(zz, count):
        block = group(zz, count)
        remote(block, block, hid_s.at[0], hid_r.at[zz], lax.rem(t + 1, T), z).wait_recv()

    def take(zz):
        pieces = [place(zz, s)[...].astype(F32) for s in range(T)]
        value = joined([unpack_rows(p) for p in pieces] if packed3 else pieces)
        mean = jnp.sum(value, axis=0, keepdims=True) * (1.0 / RP)
        d = value - mean
        hid[pl.ds(pl.multiple_of(zz * RP, 16), RP), :] = value.astype(BF16)
        st3[zz] = jnp.concatenate([mean, jnp.sum(d * d, axis=0, keepdims=True)], axis=0)

    def arrival(zz):
        @pl.when(zz == z)
        def _():
            arrived(zz, T - 1)

        @pl.when(zz != z)
        def _():
            arrived(zz, T)

    def collect(n):
        zz = lax.rem(z + n, R)
        arrival(zz)
        take(zz)

    if R == 4:
        arrived(z, T - 1)
        take(z)
        for here, order in ((0, (1, 2, 3)), (1, (2, 0, 3)), (2, (1, 3, 0)), (3, (2, 1, 0))):
            @pl.when(z == here)
            def _():
                for zz in order:
                    arrived(zz, T)
                    take(zz)
    else:
        each(R, collect)

    means = [st3[r, 0:1, :] for r in range(R)]
    mean = group_sum(functools.reduce(lambda a, b: a + b, means), member) / (per * R)
    spread = functools.reduce(lambda a, b: a + b, [st3[r, 1:2, :] for r in range(R)])
    for m in means:
        d = m - mean
        spread = spread + RP * (d * d)
    var = group_sum(spread, member) / (entries * R)
    scale3 = lax.rsqrt(var + EPS) * flat(g3)
    shift3 = flat(s3)

    def normalise(r):
        part = pl.ds(pl.multiple_of(r * RP, 16), RP)
        normed[part, :] = ((hid[part, :].astype(F32) - mean) * scale3 + shift3).astype(BF16)

    each(R, normalise)
    mine = pl.ds(pl.multiple_of(z * RP, 16), RP)
    queries = jnp.dot(normed[mine, :], mix[0], preferred_element_type=F32).astype(BF16)
    scores = lax.dot_general(queries, normed[...], NT, preferred_element_type=F32)
    peak = jnp.max(scores, axis=1, keepdims=True)
    weights = jnp.exp(scores - peak)
    total = jnp.sum(weights, axis=1, keepdims=True)
    summed = jnp.dot(weights.astype(BF16), normed[...], preferred_element_type=F32)
    attended = (summed / total).astype(BF16)
    hidden = hid[mine, :].astype(F32)
    out[...] = (hidden + jnp.dot(attended, mix[1], preferred_element_type=F32)).astype(BF16)

    most = hfull.at[pl.ds(0, N - 1)]
    remote(most, most, hid_s.at[0], hid_r.at[z], sib, z).wait_send()


def solution(mesh):
    T, R = mesh.shape["tm"], mesh.shape["rows"]

    def per_device(features, g1, s1, k1, b1, g2, s2, k2, b2, g3, s3, wq, wk, wv, wo):
        _, rows, W, C = features.shape
        OUT = k1.shape[0]
        RP, EXT, N = rows * W, (rows + 2) * W, T * R
        taps = lambda k: jnp.transpose(k, (1, 2, 3, 0, 4))
        piece = 80 if OUT == 96 and RP == 96 else RP
        vmem = pl.BlockSpec(memory_space=pltpu.VMEM)
        hbm = pl.BlockSpec(memory_space=pltpu.HBM)
        dma = pltpu.SemaphoreType.DMA
        result = pl.pallas_call(
            functools.partial(kernel, T, R, W, rows, C, OUT),
            out_shape=pltpu.VMEM((RP, C), BF16),
            in_specs=[hbm] * 15,
            out_specs=vmem,
            scratch_shapes=[pltpu.VMEM((RP, C), BF16)] + [pltpu.VMEM((C,), F32)] * 6
            + [pltpu.VMEM((OUT,), F32)] * 2 + [
                pltpu.VMEM((T, EXT, C), BF16),
                pltpu.VMEM((T, 3 if T == 4 and OUT == 96 else T, EXT, LANES), BF16),
                pltpu.VMEM((T, EXT, 3 * C), BF16),
                pltpu.VMEM((3, 3, LANES, 3 * C), BF16),
                pltpu.VMEM((3, 3, LANES, 3 * C), BF16),
                pltpu.VMEM((4, C, C), BF16),
                pltpu.VMEM((N, 2, C), F32),
                pltpu.VMEM((N, 2, T, LANES), F32),
                pltpu.VMEM((R, 2, C), F32),
                pltpu.VMEM((T, piece, LANES), BF16),
                pltpu.VMEM((N, piece, LANES), BF16),
                pltpu.VMEM((R * RP, C), BF16),
                pltpu.VMEM((R * RP, C), BF16),
                pltpu.VMEM((2, C, C), BF16),
                pltpu.VMEM((T * RP, 2 * LANES), F32),
                pltpu.VMEM((max(T - 2, 1) * RP, LANES), F32),
                dma((12,)), dma((2, 3)), dma((2, 3, T)), dma((2,)), dma((2,)), dma((1,)), dma((R,)),
            ],
            compiler_params=pltpu.CompilerParams(
                collective_id=0, has_side_effects=True, vmem_limit_bytes=62 * 1024 * 1024),
        )(features.reshape(RP, C), g1, s1, taps(k1), b1, g2, s2,
          taps(k2), b2, g3, s3, wq, wk, wv, wo)
        return result.reshape(features.shape)

    in_specs = (
        P(("clips", "tm"), "rows", None, None), P(), P(),
        P("tm", None, None, None, None), P("tm"), P(), P(),
        P("tm", None, None, None, None), P("tm"), P(), P(), P(), P(), P(), P(),
    )
    return jax.shard_map(
        per_device, mesh=mesh, in_specs=in_specs,
        out_specs=P(("clips", "tm"), "rows", None, None), check_vma=False)
```

time: 39.2 us -> 34.5 us (0.88)
  Pallas kernels: 38.4 us -> 33.7 us
    pallas_call x1, Pallas kernels: 38.4 us -> 33.7 us  [per_device(): pl.pallas_call(functools.partial(kernel, T, R, W, rows, C, OUT), out_shap...]
where the time goes in v2:
time: 34.5 us; the launch traced here: 34.3 us
  Pallas kernels  33.7 us (98%)
  local copies, waits for them, and re-layouts  0.64 us (2%)
    pallas_call x1, Pallas kernels, per_device(): pl.pallas_call(functools.partial(kernel, T, R, W, rows, C, OUT), out_shap...  33.7 us

profile of v2, /device:TPU:0, one launch (start us, length us, event | category | flops | bytes accessed | tf_op | source)
XLA Modules:
  0.0 34.3 jit_solution(12986659201093981061)
XLA Ops:
  0.0 33.7 %shard_map.145 = bf16[96,384]{1,0:T(8,128)(2,1)S(1)} custom-call(bf16[96,384]{1,0:T(8,128)(2,1)} %bitcast.7, f32[384]{0:T(512)} %g1h.1, f32[384]{0:T(512)} %s1h.1, bf16[3,3,3,96,384]{4,3,2,1,0:T(8,128)(2,1)} %bitcast.5, f32[96]{0:T(128)} %b1h.1, f32[384]{0:T(512)} %g2h.1, f32[384]{0:T(512)} %s2h.1, bf16[3,3,3,96,384]{4,3,2,1,0:T(8,128)(2,1)} %bitcast.6, ...), custom_call_target="tpu_custom_call" | custom-call | tf_op jit(solution)/shard_map/pallas_call | solution.py:537
  33.7 0.6 %copy.17 = bf16[1,2,48,384]{3,2,1,0:T(8,128)(2,1)} copy(bf16[1,2,48,384]{3,2,1,0:T(8,128)(2,1)S(1)} %bitcast.4) | data formatting | bytes 147456

commit v3 on v2

--- a/solution.py
+++ b/solution.py
@@ -76,28 +76,47 @@
 
 
 def pack_rows(v):
-    tail = v[80:96]
-    lane = lanes_of(16)
+    tail = v[72:96]
+    lane = lanes_of(24)
     parts = []
     for j in range(3):
         moved = pltpu.roll(tail, 96 - 32 * j, 1)
-        parts.append(jnp.where(lane >= 96, moved, v[16 * j : 16 * j + 16]))
-    return jnp.concatenate(parts + [v[48:80]], axis=0)
+        parts.append(jnp.where(lane >= 96, moved, v[24 * j : 24 * j + 24]))
+    return jnp.concatenate(parts, axis=0)
 
 
 def unpack_rows(p):
-    lane = lanes_of(16)
-    tail = jnp.zeros((16, LANES), F32)
+    lane = lanes_of(24)
+    tail = jnp.zeros((24, LANES), F32)
     for j in range(3):
-        moved = pltpu.roll(p[16 * j : 16 * j + 16], 32 + 32 * j, 1)
+        moved = pltpu.roll(p[24 * j : 24 * j + 24], 32 + 32 * j, 1)
         tail = jnp.where((lane >= 32 * j) & (lane < 32 * j + 32), moved, tail)
     return jnp.concatenate([p, tail], axis=0)
+
+
+def iota2(shape, axis):
+    return lax.broadcasted_iota(jnp.int32, shape, axis)
+
+
+def ones_where(mask):
+    return jnp.where(mask, 1.0, 0.0).astype(BF16)
+
+
+def merge_compact(blocks, entries):
+    count = len(blocks)
+    mean = functools.reduce(lambda a, b: a + b, blocks) / count
+    total = functools.reduce(lambda a, b: a + b, blocks)
+    for b in blocks:
+        d = pltpu.roll(b - mean, GROUPS, 1)
+        total = total + entries * (d * d)
+    inv = lax.rsqrt(total / (count * entries) + EPS)
+    return jnp.where(iota2(mean.shape, 1) < GROUPS, mean, inv)
 
 
 def kernel(T, R, W, rows, C, OUT,
            feath, g1h, s1h, w1h, b1h, g2h, s2h, w2h, b2h, g3h, s3h, wqh, wkh, wvh, woh,
            out,
-           feat, g1, s1, g2, s2, g3, s3, b1, b2, xin, y1, cols, w1, w2, aw, st1, st2, st3, hs, hfull, hid, normed, mix, pairs, singles,
+           feat, g1, s1, g2, s2, g3, s3, b1, b2, xin, y1, cols, w1, w2, aw, st1, st2, st3, hs, hfull, hid, normed, mix, spread1, spread2, norms,
            lsem, snd, rcv, st_s, st_r, hid_s, hid_r):
     t = lax.axis_index("tm")
     z = lax.axis_index("rows")
@@ -155,7 +174,9 @@
     x = feat[...].astype(F32)
     member = membership(C, per)
     mean, square = block_stats([x], member, entries)
-    st1[me] = jnp.concatenate([mean, square], axis=0)
+    first = ones_where(iota2((C, LANES), 0) == per * lax.rem(iota2((C, LANES), 1), GROUPS))
+    both = group_sum(jnp.concatenate([mean, square], axis=0), first)
+    st1[me] = jnp.where(iota2((1, LANES), 1) < GROUPS, both[0:1], both[1:2])
     for load in small[1:]:
         load.wait()
     if OUT < LANES:
@@ -251,26 +272,20 @@
         cols[f, pl.ds(offset, count), C : 2 * C] = active.astype(BF16)
         cols[f, pl.ds(offset, count), 2 * C : 3 * C] = after.astype(BF16)
 
-    def conv(weights, taps, before):
-        pair, single = before
-        for j in taps:
-            window = cols[:, j * W : j * W + RP, :].reshape(T * RP, 3 * C)
-            term = lax.dot_general(
-                window, weights[j, 0:2].reshape(2 * LANES, 3 * C), NT, preferred_element_type=F32)
-            pair = term if pair is None else pair + term
-            if T > 2:
-                term = lax.dot_general(
-                    window[: (T - 2) * RP], weights[j, 2], NT, preferred_element_type=F32)
-                single = term if single is None else single + term
-        return pair, single
-
-    def keep(sums):
-        pairs[...] = sums[0]
-        if T > 2:
-            singles[...] = sums[1]
-
-    def kept():
-        return pairs[...], (singles[...] if T > 2 else None)
+    def conv(weights, taps):
+        def stacked(parts):
+            return parts[0] if len(parts) == 1 else jnp.concatenate(parts, axis=1)
+
+        window = stacked([cols[:, j * W : j * W + RP, :].reshape(T * RP, 3 * C) for j in taps])
+        both = stacked([weights[j, 0:2].reshape(2 * LANES, 3 * C) for j in taps])
+        pair = lax.dot_general(window, both, NT, preferred_element_type=F32)
+        if T <= 2:
+            return pair, None
+        last = stacked([weights[j, 2] for j in taps])
+        return pair, lax.dot_general(window[: (T - 2) * RP], last, NT, preferred_element_type=F32)
+
+    def both_parts(weights):
+        return conv(weights, (0, 1, 2))
 
     def conv_frames(pair, single):
         results = []
@@ -290,15 +305,21 @@
     each(N - 1, lambda n: stat_copy(0, st1, n).start())
     gather_start(0, feat, feat.at[pl.ds(0, W), :], feat.at[pl.ds(RP - W, W), :], at1)
     xin[t, W : W + RP, :] = feat[...]
+    lane1 = iota2((LANES, C), 0)
+    spread1[...] = ones_where((lax.rem(lane1, GROUPS) == iota2((LANES, C), 1) // per) & (lane1 < 2 * GROUPS))
     stat_all(0, st1).wait_recv()
 
     gain1, shift1 = flat(g1), flat(s1)
+    merged = jnp.concatenate(
+        [merge_compact([st1[f * R + r] for r in range(R)], entries) for f in range(T)], axis=0)
+    low = iota2((T, LANES), 1) < GROUPS
+    wide = group_sum(
+        jnp.concatenate([jnp.where(low, merged, 0.0), jnp.where(low, 0.0, merged)], axis=0), spread1[...])
+    for f in range(T):
+        norms[f] = jnp.concatenate([wide[f : f + 1], wide[T + f : T + f + 1] * gain1], axis=0)
 
     def norm1(f):
-        means = [st1[f * R + r, 0:1, :] for r in range(R)]
-        squares = [st1[f * R + r, 1:2, :] for r in range(R)]
-        mean, inv = merge_stats(means, squares, entries)
-        return mean, inv * gain1
+        return norms[f, 0:1, :], norms[f, 1:2, :]
 
     def fill1(f, offset, count):
         mean, scale = norm1(f)
@@ -316,7 +337,6 @@
         fill1(other(n), W, RP)
 
     taps_loaded(w1, 9)
-    keep(conv(w1, (1,), (None, None)))
 
     @pl.when(z > 0)
     def _():
@@ -341,7 +361,7 @@
             cols[f, W + RP : EXT, :] = zero_row
 
     bias1 = padded(b1)
-    acc = conv(w1, (0, 2), kept())
+    acc = both_parts(w1)
     outs = [(v + bias1).astype(BF16).astype(F32) for v in conv_frames(*acc)]
     member_out = membership(LANES, per)
     if packed2:
@@ -355,11 +375,15 @@
 
     at2 = lambda src, offset, count: y1.at[src, :, pl.ds(offset, count), :]
     many2 = lambda count, offset, size: y1.at[pl.ds(0, count), :, pl.ds(offset, size), :]
+    gather_start(1, at2(t, W, RP), at2(t, W, W), at2(t, RP, W), at2)
     mean, square = block_stats(outs, member_out, entries)
-    st2[me, 0] = mean
-    st2[me, 1] = square
+    held = OUT // per
+    lane2 = iota2((LANES, LANES), 1)
+    first = ones_where(iota2((LANES, LANES), 0) == per * lax.rem(lane2, held))
+    both = group_sum(jnp.concatenate([mean, square], axis=0), first)
+    chosen = iota2((2 * T, LANES), 1) // held == iota2((2 * T, LANES), 0)
+    st2[me] = jnp.sum(jnp.where(chosen, both, 0.0), axis=0, keepdims=True)
     each(N - 1, lambda n: stat_copy(1, st2, n).start())
-    gather_start(1, at2(t, W, RP), at2(t, W, W), at2(t, RP, W), at2)
 
     pick = jnp.where(
         (lax.broadcasted_iota(jnp.int32, (C, LANES), 0)
@@ -370,16 +394,20 @@
     mix[0] = (lax.dot_general(aw[0], aw[1], NT, preferred_element_type=F32) * C ** (-0.5)).astype(BF16)
     mix[1] = jnp.dot(aw[2], aw[3], preferred_element_type=F32).astype(BF16)
 
+    for s in range(T):
+        lane3, column = iota2((LANES, C), 0), iota2((LANES, C), 1)
+        spread2[s * LANES : (s + 1) * LANES, :] = ones_where(
+            (column // OUT == s) & (lax.rem(lane3, held) == lax.rem(column, OUT) // per))
+    relay_rims(1, at2, (0,))
+    relay(1, at2, BLK, range(1, X))
+    relay_rims(1, at2, range(1, X))
     stat_all(1, st2).wait_recv()
     gain2, shift2 = flat(g2), flat(s2)
-    mean_cols, inv_cols = [], []
-    for s in range(T):
-        mean, inv = merge_stats(
-            [st2[s * R + r, 0] for r in range(R)], [st2[s * R + r, 1] for r in range(R)], entries)
-        mean_cols.append(mean[:, :OUT])
-        inv_cols.append(inv[:, :OUT])
-    mean2 = jnp.concatenate(mean_cols, axis=1)
-    scale2 = jnp.concatenate(inv_cols, axis=1) * gain2
+    holds = iota2((2 * T, LANES), 1) // held == iota2((2 * T, LANES), 0)
+    merged = jnp.concatenate(
+        [jnp.where(holds, merge_compact([st2[s * R + r] for r in range(R)], entries), 0.0) for s in range(T)], axis=1)
+    wide = group_sum(merged, spread2[...])
+    mean2, scale2 = wide[:T], wide[T:] * gain2
 
     def joined(blocks):
         return jnp.concatenate([b[:, :OUT] for b in blocks], axis=1)
@@ -399,14 +427,10 @@
         value = (raw - mean2[f : f + 1]) * scale2[f : f + 1] + shift2
         put_columns(f, offset, value)
 
-    relay_rims(1, at2, (0,))
-    relay(1, at2, BLK, range(1, X))
-    relay_rims(1, at2, range(1, X))
     sibling_wait(1, at2, BLK)
     for f in range(T):
         fill2(f, W, RP)
     taps_loaded(w2, 10)
-    keep(conv(w2, (1,), (None, None)))
 
     @pl.when(z > 0)
     def _():
@@ -421,7 +445,7 @@
             fill2(f, W + RP, W)
 
     bias2 = padded(b2)
-    acc = conv(w2, (0, 2), kept())
+    acc = both_parts(w2)
     for f, v in enumerate(conv_frames(*acc)):
         rounded = (v + bias2).astype(BF16).astype(F32)
         value = own[f * RP : (f + 1) * RP] + rounded
@@ -530,7 +554,7 @@
         OUT = k1.shape[0]
         RP, EXT, N = rows * W, (rows + 2) * W, T * R
         taps = lambda k: jnp.transpose(k, (1, 2, 3, 0, 4))
-        piece = 80 if OUT == 96 and RP == 96 else RP
+        piece = 72 if OUT == 96 and RP == 96 else RP
         vmem = pl.BlockSpec(memory_space=pltpu.VMEM)
         hbm = pl.BlockSpec(memory_space=pltpu.HBM)
         dma = pltpu.SemaphoreType.DMA
@@ -547,16 +571,17 @@
                 pltpu.VMEM((3, 3, LANES, 3 * C), BF16),
                 pltpu.VMEM((3, 3, LANES, 3 * C), BF16),
                 pltpu.VMEM((4, C, C), BF16),
-                pltpu.VMEM((N, 2, C), F32),
-                pltpu.VMEM((N, 2, T, LANES), F32),
+                pltpu.VMEM((N, 1, LANES), F32),
+                pltpu.VMEM((N, 1, LANES), F32),
                 pltpu.VMEM((R, 2, C), F32),
                 pltpu.VMEM((T, piece, LANES), BF16),
                 pltpu.VMEM((N, piece, LANES), BF16),
                 pltpu.VMEM((R * RP, C), BF16),
                 pltpu.VMEM((R * RP, C), BF16),
                 pltpu.VMEM((2, C, C), BF16),
-                pltpu.VMEM((T * RP, 2 * LANES), F32),
-                pltpu.VMEM((max(T - 2, 1) * RP, LANES), F32),
+                pltpu.VMEM((LANES, C), BF16),
+                pltpu.VMEM((T * LANES, C), BF16),
+                pltpu.VMEM((T, 2, C), F32),
                 dma((12,)), dma((2, 3)), dma((2, 3, T)), dma((2,)), dma((2,)), dma((1,)), dma((R,)),
             ],
             compiler_params=pltpu.CompilerParams(

time: 34.5 us -> 32.1 us (0.930)
  Pallas kernels: 33.7 us -> 31.3 us
    pallas_call x1, Pallas kernels: 33.7 us -> 31.3 us  [per_device(): pl.pallas_call(functools.partial(kernel, T, R, W, rows, C, OUT), out_shap...]
where the time goes in v3:
time: 32.1 us; the launch traced here: 32 us
  Pallas kernels  31.3 us (98%)
  local copies, waits for them, and re-layouts  0.64 us (2%)
    pallas_call x1, Pallas kernels, per_device(): pl.pallas_call(functools.partial(kernel, T, R, W, rows, C, OUT), out_shap...  31.3 us

profile of v3, /device:TPU:0, one launch (start us, length us, event | category | flops | bytes accessed | tf_op | source)
XLA Modules:
  0.0 32.0 jit_solution(17924149057291998228)
XLA Ops:
  0.0 31.3 %shard_map.145 = bf16[96,384]{1,0:T(8,128)(2,1)S(1)} custom-call(bf16[96,384]{1,0:T(8,128)(2,1)} %bitcast.7, f32[384]{0:T(512)} %g1h.1, f32[384]{0:T(512)} %s1h.1, bf16[3,3,3,96,384]{4,3,2,1,0:T(8,128)(2,1)} %bitcast.5, f32[96]{0:T(128)} %b1h.1, f32[384]{0:T(512)} %g2h.1, f32[384]{0:T(512)} %s2h.1, bf16[3,3,3,96,384]{4,3,2,1,0:T(8,128)(2,1)} %bitcast.6, ...), custom_call_target="tpu_custom_call" | custom-call | tf_op jit(solution)/shard_map/pallas_call | solution.py:561
  31.3 0.6 %copy.17 = bf16[1,2,48,384]{3,2,1,0:T(8,128)(2,1)} copy(bf16[1,2,48,384]{3,2,1,0:T(8,128)(2,1)S(1)} %bitcast.4) | data formatting | bytes 147456

commit v4 on v3

--- a/solution.py
+++ b/solution.py
@@ -307,6 +307,9 @@
     xin[t, W : W + RP, :] = feat[...]
     lane1 = iota2((LANES, C), 0)
     spread1[...] = ones_where((lax.rem(lane1, GROUPS) == iota2((LANES, C), 1) // per) & (lane1 < 2 * GROUPS))
+    relay(0, at1, BLK, range(1, X))
+    relay_rims(0, at1, (0,))
+    relay_rims(0, at1, range(1, X))
     stat_all(0, st1).wait_recv()
 
     gain1, shift1 = flat(g1), flat(s1)
@@ -327,11 +330,8 @@
         put_columns(f, offset, value)
 
     fill1(t, W, RP)
-    relay(0, at1, BLK, range(1, X))
     for n in range(1, X):
         fill1(same(n), W, RP)
-    relay_rims(0, at1, (0,))
-    relay_rims(0, at1, range(1, X))
     sibling_wait(0, at1, BLK)
     for n in range(X):
         fill1(other(n), W, RP)
@@ -460,11 +460,11 @@
     def hidden_start(pt, pz):
         remote(hs.at[pt], place(z, t), hid_s.at[0], hid_r.at[z], pt, pz).start()
 
-    if R <= 4:
-        for d in range(R - 1, 0, -1):
-            for there in (z + d, z - d):
-                @pl.when((there >= 0) & (there < R))
-                def _():
+    if R == 4:
+        for here, order in ((0, (2, 1)), (1, (0, 2, 3)), (2, (0, 1, 3)), (3, (0, 2))):
+            @pl.when(z == here)
+            def _():
+                for there in order:
                     for n in range(T):
                         hidden_start(lax.rem(t + n, T), there)
         for n in range(1, T):
@@ -482,47 +482,51 @@
         block = group(zz, count)
         remote(block, block, hid_s.at[0], hid_r.at[zz], lax.rem(t + 1, T), z).wait_recv()
 
-    def take(zz):
+    def block_of(zz):
         pieces = [place(zz, s)[...].astype(F32) for s in range(T)]
-        value = joined([unpack_rows(p) for p in pieces] if packed3 else pieces)
-        mean = jnp.sum(value, axis=0, keepdims=True) * (1.0 / RP)
-        d = value - mean
+        return joined([unpack_rows(p) for p in pieces] if packed3 else pieces)
+
+    def take(zz, centre, value=None):
+        value = block_of(zz) if value is None else value
+        d = value - centre
         hid[pl.ds(pl.multiple_of(zz * RP, 16), RP), :] = value.astype(BF16)
-        st3[zz] = jnp.concatenate([mean, jnp.sum(d * d, axis=0, keepdims=True)], axis=0)
-
-    def arrival(zz):
-        @pl.when(zz == z)
-        def _():
-            arrived(zz, T - 1)
-
-        @pl.when(zz != z)
-        def _():
-            arrived(zz, T)
-
-    def collect(n):
-        zz = lax.rem(z + n, R)
-        arrival(zz)
-        take(zz)
+        st3[...] += jnp.concatenate(
+            [jnp.sum(d, axis=0, keepdims=True), jnp.sum(d * d, axis=0, keepdims=True)], axis=0)
+
+    def forwarded(zz):
+        return remote(group(zz, T), group(zz, T), hid_s.at[1 + zz // 3], hid_r.at[zz], t, 3 - zz * 2 // 3)
 
     if R == 4:
-        arrived(z, T - 1)
-        take(z)
-        for here, order in ((0, (1, 2, 3)), (1, (2, 0, 3)), (2, (1, 3, 0)), (3, (2, 1, 0))):
+        for here, source in ((2, 3), (2, 0)):
+            @pl.when(z == here)
+            def _():
+                arrived(source, T)
+                forwarded(source).start()
+
+    st3[...] = jnp.zeros((2, C), F32)
+    arrived(z, T - 1)
+    mine_now = block_of(z)
+    centre = group_sum(jnp.sum(mine_now, axis=0, keepdims=True), member) / entries
+    take(z, centre, mine_now)
+    if R == 4:
+        for here, order in ((0, (1, 2, 3)), (1, (3, 0, 2)), (2, (0, 3, 1)), (3, (2, 1, 0))):
             @pl.when(z == here)
             def _():
                 for zz in order:
-                    arrived(zz, T)
-                    take(zz)
+                    if (here, zz) not in ((2, 0), (2, 3)):
+                        arrived(zz, T)
+                    take(zz, centre)
     else:
-        each(R, collect)
-
-    means = [st3[r, 0:1, :] for r in range(R)]
-    mean = group_sum(functools.reduce(lambda a, b: a + b, means), member) / (per * R)
-    spread = functools.reduce(lambda a, b: a + b, [st3[r, 1:2, :] for r in range(R)])
-    for m in means:
-        d = m - mean
-        spread = spread + RP * (d * d)
-    var = group_sum(spread, member) / (entries * R)
+        def collect(n):
+            zz = lax.rem(z + n + 1, R)
+            arrived(zz, T)
+            take(zz, centre)
+
+        each(R - 1, collect)
+
+    moments = group_sum(st3[...], member) / (entries * R)
+    mean = centre + moments[0:1]
+    var = moments[1:2] - moments[0:1] * moments[0:1]
     scale3 = lax.rsqrt(var + EPS) * flat(g3)
     shift3 = flat(s3)
 
@@ -538,12 +542,28 @@
     weights = jnp.exp(scores - peak)
     total = jnp.sum(weights, axis=1, keepdims=True)
     summed = jnp.dot(weights.astype(BF16), normed[...], preferred_element_type=F32)
-    attended = (summed / total).astype(BF16)
-    hidden = hid[mine, :].astype(F32)
-    out[...] = (hidden + jnp.dot(attended, mix[1], preferred_element_type=F32)).astype(BF16)
-
-    most = hfull.at[pl.ds(0, N - 1)]
-    remote(most, most, hid_s.at[0], hid_r.at[z], sib, z).wait_send()
+    projected = jnp.dot(summed.astype(BF16), mix[1], preferred_element_type=F32)
+    out[...] = (hid[mine, :].astype(F32) + projected / total).astype(BF16)
+
+    def hidden_sent(count):
+        most = hfull.at[pl.ds(0, count)]
+        remote(most, most, hid_s.at[0], hid_r.at[z], sib, z).wait_send()
+
+    if R == 4:
+        for here, source in ((2, 3), (2, 0)):
+            @pl.when(z == here)
+            def _():
+                forwarded(source).wait_send()
+
+        @pl.when((z == 0) | (z == 3))
+        def _():
+            hidden_sent(N - 1 - T)
+
+        @pl.when((z == 1) | (z == 2))
+        def _():
+            hidden_sent(N - 1)
+    else:
+        hidden_sent(N - 1)
 
 
 def solution(mesh):
@@ -573,7 +593,7 @@
                 pltpu.VMEM((4, C, C), BF16),
                 pltpu.VMEM((N, 1, LANES), F32),
                 pltpu.VMEM((N, 1, LANES), F32),
-                pltpu.VMEM((R, 2, C), F32),
+                pltpu.VMEM((2, C), F32),
                 pltpu.VMEM((T, piece, LANES), BF16),
                 pltpu.VMEM((N, piece, LANES), BF16),
                 pltpu.VMEM((R * RP, C), BF16),
@@ -582,7 +602,7 @@
                 pltpu.VMEM((LANES, C), BF16),
                 pltpu.VMEM((T * LANES, C), BF16),
                 pltpu.VMEM((T, 2, C), F32),
-                dma((12,)), dma((2, 3)), dma((2, 3, T)), dma((2,)), dma((2,)), dma((1,)), dma((R,)),
+                dma((12,)), dma((2, 3)), dma((2, 3, T)), dma((2,)), dma((2,)), dma((3,)), dma((R,)),
             ],
             compiler_params=pltpu.CompilerParams(
                 collective_id=0, has_side_effects=True, vmem_limit_bytes=62 * 1024 * 1024),

time: 32.1 us -> 31.8 us (level)
  no operation moved by 1% of the time
where the time goes in v4:
time: 31.8 us; the launch traced here: 31.7 us
  Pallas kernels  31 us (97%)
  local copies, waits for them, and re-layouts  0.64 us (2%)
    pallas_call x1, Pallas kernels, per_device(): pl.pallas_call(functools.partial(kernel, T, R, W, rows, C, OUT), out_shap...  31 us

profile of v4, /device:TPU:0, one launch (start us, length us, event | category | flops | bytes accessed | tf_op | source)
XLA Modules:
  0.0 31.7 jit_solution(924675794523149921)
XLA Ops:
  0.0 31.0 %shard_map.145 = bf16[96,384]{1,0:T(8,128)(2,1)S(1)} custom-call(bf16[96,384]{1,0:T(8,128)(2,1)} %bitcast.7, f32[384]{0:T(512)} %g1h.1, f32[384]{0:T(512)} %s1h.1, bf16[3,3,3,96,384]{4,3,2,1,0:T(8,128)(2,1)} %bitcast.5, f32[96]{0:T(128)} %b1h.1, f32[384]{0:T(512)} %g2h.1, f32[384]{0:T(512)} %s2h.1, bf16[3,3,3,96,384]{4,3,2,1,0:T(8,128)(2,1)} %bitcast.6, ...), custom_call_target="tpu_custom_call" | custom-call | tf_op jit(solution)/shard_map/pallas_call | solution.py:581
  31.1 0.6 %copy.17 = bf16[1,2,48,384]{3,2,1,0:T(8,128)(2,1)} copy(bf16[1,2,48,384]{3,2,1,0:T(8,128)(2,1)S(1)} %bitcast.4) | data formatting | bytes 147456

commit v5 on v4

--- a/solution.py
+++ b/solution.py
@@ -146,7 +146,23 @@
             (b1h, b1), (b2h, b2)))
     ]
     small[0].start()
-    each(N - 1, greet)
+    chained = R == 4
+
+    def at_row(here):
+        return pl.when(z == here)
+
+    def row_greet(here):
+        rows_of = [here] + [zz for zz in range(R) if zz > here or zz == here - 1 or (here, zz) == (2, 0)]
+        for zz in rows_of:
+            for n in range(1 if zz == here else 0, T):
+                pl.semaphore_signal(
+                    barrier, inc=1, device_id={"tm": lax.rem(t + n, T), "rows": zz}, device_id_type=MESH)
+
+    if chained:
+        for here in range(R):
+            at_row(here)(functools.partial(row_greet, here))
+    else:
+        each(N - 1, greet)
     for load in small[1:]:
         load.start()
 
@@ -183,7 +199,10 @@
         w1[:, :, OUT:, :] = jnp.zeros((3, 3, LANES - OUT, 3 * C), BF16)
         w2[:, :, OUT:, :] = jnp.zeros((3, 3, LANES - OUT, 3 * C), BF16)
 
-    pl.semaphore_wait(barrier, N - 1)
+    if chained:
+        pl.semaphore_wait(barrier, 3 * T - 1 + T * (z // 2))
+    else:
+        pl.semaphore_wait(barrier, N - 1)
 
     def stat_copy(phase, ref, n):
         pt, pz = peer(n + 1)
@@ -302,15 +321,54 @@
 
     at1 = lambda src, offset, count: xin.at[src, pl.ds(offset, count), :]
     many1 = lambda count, offset, size: xin.at[pl.ds(0, count), pl.ds(offset, size), :]
-    each(N - 1, lambda n: stat_copy(0, st1, n).start())
+    targets_of = ((0, 1, 2), (1, 0, 2), (2, 0, 1), (3, 0, 1, 2))
+
+    def row_sends(here):
+        for zz in targets_of[here]:
+            for n in range(1 if zz == here else 0, T):
+                sem = 2 if n == 0 and here < 2 and zz == 2 else 0
+                remote(st1.at[me], st1.at[me], st_s.at[0], st_r.at[sem], lax.rem(t + n, T), zz).start()
+
+    def column(count):
+        return st1.at[pl.ds(t * R, count)]
+
+    def pass_up(here):
+        remote(column(2), column(2), st_s.at[2], st_r.at[2], sib, z).wait_recv()
+        for n in range(T):
+            remote(column(3), column(3), st_s.at[2], st_r.at[0], lax.rem(t + n, T), 3).start()
+
+    def row_stats(here):
+        most = st1.at[pl.ds(0, N - 3 if here == 2 else N - 1)]
+        remote(most, most, st_s.at[0], st_r.at[0], sib, z).wait_recv()
+
+    def row_sent(here):
+        most = st1.at[pl.ds(0, T * len(targets_of[here]) - 1)]
+        remote(most, most, st_s.at[0], st_r.at[0], sib, z).wait_send()
+        if here == 2:
+            most = st1.at[pl.ds(0, 3 * T)]
+            remote(most, most, st_s.at[2], st_r.at[0], sib, z).wait_send()
+
+    def by_row(body, which):
+        for here in which:
+            at_row(here)(functools.partial(body, here))
+
+    if chained:
+        by_row(row_sends, range(R))
+    else:
+        each(N - 1, lambda n: stat_copy(0, st1, n).start())
     gather_start(0, feat, feat.at[pl.ds(0, W), :], feat.at[pl.ds(RP - W, W), :], at1)
     xin[t, W : W + RP, :] = feat[...]
     lane1 = iota2((LANES, C), 0)
     spread1[...] = ones_where((lax.rem(lane1, GROUPS) == iota2((LANES, C), 1) // per) & (lane1 < 2 * GROUPS))
+    if chained:
+        by_row(pass_up, (2,))
     relay(0, at1, BLK, range(1, X))
     relay_rims(0, at1, (0,))
     relay_rims(0, at1, range(1, X))
-    stat_all(0, st1).wait_recv()
+    if chained:
+        by_row(row_stats, range(R))
+    else:
+        stat_all(0, st1).wait_recv()
 
     gain1, shift1 = flat(g1), flat(s1)
     merged = jnp.concatenate(
@@ -473,7 +531,10 @@
         each(N - 1, lambda n: hidden_start(*peer(n + 1)))
     hfull[z * T + t] = hs[t]
 
-    stat_all(0, st1).wait_send()
+    if chained:
+        by_row(row_sent, range(R))
+    else:
+        stat_all(0, st1).wait_send()
     gather_sent(0, at1, many1)
     stat_all(1, st2).wait_send()
     gather_sent(1, at2, many2)
@@ -602,7 +663,7 @@
                 pltpu.VMEM((LANES, C), BF16),
                 pltpu.VMEM((T * LANES, C), BF16),
                 pltpu.VMEM((T, 2, C), F32),
-                dma((12,)), dma((2, 3)), dma((2, 3, T)), dma((2,)), dma((2,)), dma((3,)), dma((R,)),
+                dma((12,)), dma((2, 3)), dma((2, 3, T)), dma((3,)), dma((3,)), dma((3,)), dma((R,)),
             ],
             compiler_params=pltpu.CompilerParams(
                 collective_id=0, has_side_effects=True, vmem_limit_bytes=62 * 1024 * 1024),

time: 31.8 us -> 31.7 us (level)
  no operation moved by 1% of the time
where the time goes in v5:
time: 31.7 us; the launch traced here: 31.6 us
  Pallas kernels  30.9 us (97%)
  local copies, waits for them, and re-layouts  0.64 us (2%)
    pallas_call x1, Pallas kernels, per_device(): pl.pallas_call(functools.partial(kernel, T, R, W, rows, C, OUT), out_shap...  30.9 us
    unnamed x1, local copies, waits for them, and re-layouts  0.64 us

profile of v5, /device:TPU:0, one launch (start us, length us, event | category | flops | bytes accessed | tf_op | source)
XLA Modules:
  0.0 31.6 jit_solution(17089373655218392907)
XLA Ops:
  0.0 30.9 %shard_map.145 = bf16[96,384]{1,0:T(8,128)(2,1)S(1)} custom-call(bf16[96,384]{1,0:T(8,128)(2,1)} %bitcast.7, f32[384]{0:T(512)} %g1h.1, f32[384]{0:T(512)} %s1h.1, bf16[3,3,3,96,384]{4,3,2,1,0:T(8,128)(2,1)} %bitcast.5, f32[96]{0:T(128)} %b1h.1, f32[384]{0:T(512)} %g2h.1, f32[384]{0:T(512)} %s2h.1, bf16[3,3,3,96,384]{4,3,2,1,0:T(8,128)(2,1)} %bitcast.6, ...), custom_call_target="tpu_custom_call" | custom-call | tf_op jit(solution)/shard_map/pallas_call | solution.py:642
  30.9 0.6 %copy.17 = bf16[1,2,48,384]{3,2,1,0:T(8,128)(2,1)} copy(bf16[1,2,48,384]{3,2,1,0:T(8,128)(2,1)S(1)} %bitcast.4) | data formatting | bytes 147456

commit v6 on v5

--- a/solution.py
+++ b/solution.py
@@ -117,7 +117,7 @@
            feath, g1h, s1h, w1h, b1h, g2h, s2h, w2h, b2h, g3h, s3h, wqh, wkh, wvh, woh,
            out,
            feat, g1, s1, g2, s2, g3, s3, b1, b2, xin, y1, cols, w1, w2, aw, st1, st2, st3, hs, hfull, hid, normed, mix, spread1, spread2, norms,
-           lsem, snd, rcv, st_s, st_r, hid_s, hid_r):
+           lsem, snd, rcv, st_r, hid_r):
     t = lax.axis_index("tm")
     z = lax.axis_index("rows")
     me = t * R + z
@@ -206,11 +206,11 @@
 
     def stat_copy(phase, ref, n):
         pt, pz = peer(n + 1)
-        return remote(ref.at[me], ref.at[me], st_s.at[phase], st_r.at[phase], pt, pz)
+        return remote(ref.at[me], ref.at[me], lsem.at[4 + phase], st_r.at[phase], pt, pz)
 
     def stat_all(phase, ref):
         most = ref.at[pl.ds(0, N - 1)]
-        return remote(most, most, st_s.at[phase], st_r.at[phase], lax.rem(t + 1, T), z)
+        return remote(most, most, lsem.at[4 + phase], st_r.at[phase], lax.rem(t + 1, T), z)
 
     core = lax.rem(t, 2)
     sib = t + 1 - 2 * core
@@ -327,26 +327,26 @@
         for zz in targets_of[here]:
             for n in range(1 if zz == here else 0, T):
                 sem = 2 if n == 0 and here < 2 and zz == 2 else 0
-                remote(st1.at[me], st1.at[me], st_s.at[0], st_r.at[sem], lax.rem(t + n, T), zz).start()
+                remote(st1.at[me], st1.at[me], lsem.at[4], st_r.at[sem], lax.rem(t + n, T), zz).start()
 
     def column(count):
         return st1.at[pl.ds(t * R, count)]
 
     def pass_up(here):
-        remote(column(2), column(2), st_s.at[2], st_r.at[2], sib, z).wait_recv()
+        remote(column(2), column(2), lsem.at[6], st_r.at[2], sib, z).wait_recv()
         for n in range(T):
-            remote(column(3), column(3), st_s.at[2], st_r.at[0], lax.rem(t + n, T), 3).start()
+            remote(column(3), column(3), lsem.at[6], st_r.at[0], lax.rem(t + n, T), 3).start()
 
     def row_stats(here):
         most = st1.at[pl.ds(0, N - 3 if here == 2 else N - 1)]
-        remote(most, most, st_s.at[0], st_r.at[0], sib, z).wait_recv()
+        remote(most, most, lsem.at[4], st_r.at[0], sib, z).wait_recv()
 
     def row_sent(here):
         most = st1.at[pl.ds(0, T * len(targets_of[here]) - 1)]
-        remote(most, most, st_s.at[0], st_r.at[0], sib, z).wait_send()
+        remote(most, most, lsem.at[4], st_r.at[0], sib, z).wait_send()
         if here == 2:
             most = st1.at[pl.ds(0, 3 * T)]
-            remote(most, most, st_s.at[2], st_r.at[0], sib, z).wait_send()
+            remote(most, most, lsem.at[6], st_r.at[0], sib, z).wait_send()
 
     def by_row(body, which):
         for here in which:
@@ -516,7 +516,7 @@
         return hfull.at[pl.ds(zz * T, count)]
 
     def hidden_start(pt, pz):
-        remote(hs.at[pt], place(z, t), hid_s.at[0], hid_r.at[z], pt, pz).start()
+        remote(hs.at[pt], place(z, t), lsem.at[1], hid_r.at[z], pt, pz).start()
 
     if R == 4:
         for here, order in ((0, (2, 1)), (1, (0, 2, 3)), (2, (0, 1, 3)), (3, (0, 2))):
@@ -541,7 +541,7 @@
 
     def arrived(zz, count):
         block = group(zz, count)
-        remote(block, block, hid_s.at[0], hid_r.at[zz], lax.rem(t + 1, T), z).wait_recv()
+        remote(block, block, lsem.at[1], hid_r.at[zz], lax.rem(t + 1, T), z).wait_recv()
 
     def block_of(zz):
         pieces = [place(zz, s)[...].astype(F32) for s in range(T)]
@@ -555,7 +555,7 @@
             [jnp.sum(d, axis=0, keepdims=True), jnp.sum(d * d, axis=0, keepdims=True)], axis=0)
 
     def forwarded(zz):
-        return remote(group(zz, T), group(zz, T), hid_s.at[1 + zz // 3], hid_r.at[zz], t, 3 - zz * 2 // 3)
+        return remote(group(zz, T), group(zz, T), lsem.at[2 + zz // 3], hid_r.at[zz], t, 3 - zz * 2 // 3)
 
     if R == 4:
         for here, source in ((2, 3), (2, 0)):
@@ -608,7 +608,7 @@
 
     def hidden_sent(count):
         most = hfull.at[pl.ds(0, count)]
-        remote(most, most, hid_s.at[0], hid_r.at[z], sib, z).wait_send()
+        remote(most, most, lsem.at[1], hid_r.at[z], sib, z).wait_send()
 
     if R == 4:
         for here, source in ((2, 3), (2, 0)):
@@ -663,7 +663,7 @@
                 pltpu.VMEM((LANES, C), BF16),
                 pltpu.VMEM((T * LANES, C), BF16),
                 pltpu.VMEM((T, 2, C), F32),
-                dma((12,)), dma((2, 3)), dma((2, 3, T)), dma((3,)), dma((3,)), dma((3,)), dma((R,)),
+                dma((12,)), dma((2, 3)), dma((2, 3, T)), dma((3,)), dma((R,)),
             ],
             compiler_params=pltpu.CompilerParams(
                 collective_id=0, has_side_effects=True, vmem_limit_bytes=62 * 1024 * 1024),

time: 31.7 us -> 31.6 us (level)
  no operation moved by 1% of the time
where the time goes in v6:
time: 31.6 us; the launch traced here: 31.5 us
  Pallas kernels  30.9 us (98%)
  local copies, waits for them, and re-layouts  0.64 us (2%)
    pallas_call x1, Pallas kernels, per_device(): pl.pallas_call(functools.partial(kernel, T, R, W, rows, C, OUT), out_shap...  30.9 us
    unnamed x1, local copies, waits for them, and re-layouts  0.64 us

profile of v6, /device:TPU:0, one launch (start us, length us, event | category | flops | bytes accessed | tf_op | source)
XLA Modules:
  0.0 31.5 jit_solution(4021686767398309449)
XLA Ops:
  0.0 30.9 %shard_map.145 = bf16[96,384]{1,0:T(8,128)(2,1)S(1)} custom-call(bf16[96,384]{1,0:T(8,128)(2,1)} %bitcast.7, f32[384]{0:T(512)} %g1h.1, f32[384]{0:T(512)} %s1h.1, bf16[3,3,3,96,384]{4,3,2,1,0:T(8,128)(2,1)} %bitcast.5, f32[96]{0:T(128)} %b1h.1, f32[384]{0:T(512)} %g2h.1, f32[384]{0:T(512)} %s2h.1, bf16[3,3,3,96,384]{4,3,2,1,0:T(8,128)(2,1)} %bitcast.6, ...), custom_call_target="tpu_custom_call" | custom-call | tf_op jit(solution)/shard_map/pallas_call | solution.py:642
  30.9 0.6 %copy.17 = bf16[1,2,48,384]{3,2,1,0:T(8,128)(2,1)} copy(bf16[1,2,48,384]{3,2,1,0:T(8,128)(2,1)S(1)} %bitcast.4) | data formatting | bytes 147456
